TPU v7x, 256 devices: a whole 4x4x8 slice. The times are simulated.
256 devices in a mesh: tm: 8 (over z), ha: 8 (over x, core), wa: 4 (over y).
Axes of the slice: x: 4, y: 4, z: 8, core: 2. Of those that a mesh axis runs over, the one named last changes fastest.
Arguments:
- latents: bfloat16 [2, 16, 64, 32, 256], P(None, 'tm', 'ha', 'wa'), may hold values from -60 to 60, as said below
- gain_one: float32 [256], replicated, may hold values from 0.5 to 2
- shift_one: float32 [256], replicated, may hold values from -1 to 1
- kernel_one: bfloat16 [3, 3, 3, 256, 256], replicated, may hold values from -0.078125 to 0.078125
- bias_one: float32 [256], replicated, may hold values from -0.5 to 0.5
- gain_two: float32 [256], replicated, may hold values from 0.5 to 2
- shift_two: float32 [256], replicated, may hold values from -1 to 1
- kernel_two: bfloat16 [3, 3, 3, 256, 256], replicated, may hold values from -0.078125 to 0.078125
- bias_two: float32 [256], replicated, may hold values from -0.5 to 0.5
- kernel_up: bfloat16 [3, 3, 3, 256, 256], replicated, may hold values from -0.078125 to 0.078125
- bias_up: float32 [256], replicated, may hold values from -0.5 to 0.5
Outputs:
- decoded: bfloat16 [2, 16, 128, 64, 256], P(None, 'tm', 'ha', 'wa')
Inputs may be any that keep to these rules, and one draw needn't show every extreme that they name: `latents`: float activations.
All inputs are finite; a program needn't handle non-finite values.
Results may differ from a plain program's by a relative error of at most 0.014.
Values may be sent and summed in bfloat16 or wider, within the bound.
A program may use at most 64 MiB of HBM per device.

v0:
```python
import functools

import jax
import jax.numpy as jnp
from jax import lax
from jax.experimental import pallas as pl
from jax.experimental.pallas import tpu as pltpu
from jax.sharding import PartitionSpec as P

MESH = pl.DeviceIdType.MESH
AXES = ("tm", "ha", "wa")
GROUP = 8
EPS = 1e-6
F32, BF16 = jnp.float32, jnp.bfloat16
CH = 256


def lanes(shape):
    return lax.broadcasted_iota(jnp.int32, shape, len(shape) - 1)


def group_sum(x):
    lane = lanes(x.shape)
    for s in (1, 2, 4):
        x = x + jnp.where((lane // s) % 2 == 0, pltpu.roll(x, 128 - s, 1), pltpu.roll(x, s, 1))
    return x


def halves(x):
    return jnp.concatenate([x[:, :128], x[:, 128:]], axis=0)


def whole(x, clip):
    return jnp.concatenate([x[clip : clip + 1], x[2 + clip : 3 + clip]], axis=1)


def moments(tile, count):
    sums = jnp.sum(jnp.sum(tile, axis=(0, 1)), axis=1)
    mean = group_sum(halves(sums)) * (1.0 / count)
    centre = jnp.stack([whole(mean, 0), whole(mean, 1)])
    dev = tile - centre[None, None]
    spread = group_sum(halves(jnp.sum(jnp.sum(dev * dev, axis=(0, 1)), axis=1)))
    rows = jnp.concatenate([mean[0:2], spread[0:2], mean[2:4], spread[2:4]], axis=0)
    pick = lanes((8, 128)) % 8 == lax.broadcasted_iota(jnp.int32, (8, 128), 0)
    return jnp.sum(jnp.where(pick, rows, 0.0), axis=0, keepdims=True)


def merge(rows, count):
    n = rows.shape[0]
    total = jnp.sum(rows, axis=0)
    mean = total * (1.0 / n)
    dev = rows - mean[None]
    apart = jnp.sum(dev * dev, axis=0)
    return jnp.where(lanes((1, 128)) % 4 < 2, mean, total + float(count) * pltpu.roll(apart, 2, 1))


def spread_out(row, total):
    pick = lanes((8, 128)) % 8 == lax.broadcasted_iota(jnp.int32, (8, 128), 0)
    v = group_sum(jnp.where(pick, row, 0.0))
    mean = [jnp.concatenate([v[c : c + 1], v[4 + c : 5 + c]], axis=1) for c in (0, 1)]
    m2 = [jnp.concatenate([v[2 + c : 3 + c], v[6 + c : 7 + c]], axis=1) for c in (0, 1)]
    return mean, [lax.rsqrt(m * (1.0 / total) + EPS) for m in m2]


def silu(u):
    return u * (0.5 + 0.5 * jnp.tanh(0.5 * u))


def body(sizes, lat, gain1, shift1, k1, bias1, gain2, shift2, k2, bias2, ku, bias_up, out,
         xv, cb, sl, sx, xr, cp, ss, sf, ab, k1v, k2v, kuv, kuc, fbuf, acc, ob, g1, g2, g3, g4,
         lsem, ssem, rsem, gsend, grecv):
    nt, nh, nw = sizes
    it, ih, iw = (lax.axis_index(a) for a in AXES)

    def at(dt, dh, dw):
        if dh is None:
            return (it, ih + 1 - 2 * lax.rem(ih, 2), iw)
        return (lax.rem(it + dt % nt, nt), lax.rem(ih + dh % nh, nh), lax.rem(iw + dw % nw, nw))

    def ring(d, n):
        return min(d, n - d)

    plane = sorted(
        [(0, a, b) for a in range(nh) for b in range(nw) if a or b],
        key=lambda o: -(ring(o[1], nh) + 2 * ring(o[2], nw)),
    )
    line = sorted([(a, 0, 0) for a in range(1, nt)], key=lambda o: -ring(o[0], nt))

    pair = [(0, None, 0)]
    chips = sorted(
        [(a, 2 * b, c) for a in range(nt) for b in range(nh // 2) for c in range(nw) if a or b or c],
        key=lambda o: -(ring(o[0], nt) + ring(o[1], nh) // 2 + ring(o[2], nw)),
    )

    loads = [
        pltpu.make_async_copy(s, d, lsem.at[i])
        for i, (s, d) in enumerate(((lat, xv), (k1, k1v), (ku, kuv), (k2, k2v)))
    ]
    loads[0].start()
    barrier = pltpu.get_barrier_semaphore()
    for o in plane + line:
        pl.semaphore_signal(barrier, inc=1, device_id=at(*o), device_id_type=MESH)
    for c in loads[1:]:
        c.start()

    sends = []

    def send(e, slot, src, dst, offset):
        c = pltpu.make_async_remote_copy(
            src_ref=src, dst_ref=dst, send_sem=ssem.at[e, slot], recv_sem=rsem.at[e, slot],
            device_id=at(*offset), device_id_type=MESH)
        c.start()
        sends.append(c)
        return c

    def edges(e):
        for half in (0, 1):
            cols = pl.ds(half * 128, 128)
            left = fbuf[half, pl.ds(0, 32, stride=8), :]
            right = fbuf[half, pl.ds(7, 32, stride=8), :]
            ss[e, 0, :, cols] = left.astype(BF16)
            ss[e, 1, :, cols] = right.astype(BF16)
            parts = []
            for h in (0, 14):
                for side in (left, right):
                    parts += [side[h : h + 2], side[16 + h : 18 + h]]
            sx[e, :, cols] = jnp.concatenate(parts, axis=0).astype(BF16)

    def near(e):
        own = pl.ds(2, 2)
        return [
            send(e, 0, cb.at[e, own, 1], cb.at[e, own, 9], (0, -1, 0)),
            send(e, 1, cb.at[e, own, 8], cb.at[e, own, 0], (0, 1, 0)),
            send(e, 2, ss.at[e, 0], sl.at[e, 1, 1], (0, 0, -1)),
            send(e, 3, ss.at[e, 1], sl.at[e, 1, 0], (0, 0, 1)),
            send(e, 4, sx.at[e], xr.at[e, 0], (0, -1, -1)),
            send(e, 5, sx.at[e], xr.at[e, 1], (0, -1, 1)),
            send(e, 6, sx.at[e], xr.at[e, 2], (0, 1, -1)),
            send(e, 7, sx.at[e], xr.at[e, 3], (0, 1, 1)),
        ]

    def tile_on(e):
        return send(e, 8, cb.at[e, pl.ds(2, 2), pl.ds(1, 8)], cb.at[e, pl.ds(0, 2), pl.ds(1, 8)], (1, 0, 0))

    def frame_on(e, t):
        rows = pl.ds(1, 8)
        return send(e, 8 if t == 0 else 13, cb.at[e, 2 + t, rows], cb.at[e, t, rows], (1, 0, 0))

    def rims_on(e, arrivals):
        for c in arrivals:
            c.wait_recv()
        block = lax.broadcasted_iota(jnp.int32, (16, CH), 0) // 4
        tiles = [xr[e, d].astype(F32) for d in range(4)]
        picked = jnp.where(
            block == 0, tiles[0], jnp.where(block == 1, tiles[1], jnp.where(block == 2, tiles[2], tiles[3]))
        )
        cp[e, 1] = picked.astype(BF16)
        prev, own = pl.ds(0, 2), pl.ds(2, 2)
        return [
            send(e, 9, cb.at[e, own, 0], cb.at[e, prev, 0], (1, 0, 0)),
            send(e, 10, cb.at[e, own, 9], cb.at[e, prev, 9], (1, 0, 0)),
            send(e, 11, sl.at[e, 1], sl.at[e, 0], (1, 0, 0)),
            send(e, 12, cp.at[e, 1], cp.at[e, 0], (1, 0, 0)),
        ]

    def gather(e, phase, buf, row, offsets):
        buf[0] = row
        for slot, o in enumerate(offsets):
            pltpu.make_async_remote_copy(
                src_ref=buf.at[0], dst_ref=buf.at[1 + slot], send_sem=gsend.at[e, phase],
                recv_sem=grecv.at[e, phase], device_id=at(*o), device_id_type=MESH).start()

    def gathered(e, phase, buf, offsets):
        peers = buf.at[pl.ds(1, len(offsets))]
        c = pltpu.make_async_remote_copy(
            src_ref=peers, dst_ref=peers, send_sem=gsend.at[e, phase], recv_sem=grecv.at[e, phase],
            device_id=at(1, 0, 0), device_id_type=MESH)
        c.wait_recv()
        sends.append(c)
        return buf[...]

    def fill(e, frames, norm):
        lo, hi = frames
        pairs = [p for p in (0, 1) if lo <= 2 * p < hi]
        if norm is not None:
            mean, scale, shift = norm
            parity = lax.broadcasted_iota(jnp.int32, (8, CH), 0) % 2 == 0
            mean8 = jnp.where(parity, mean[0], mean[1])
            scale8 = jnp.where(parity, scale[0], scale[1])
            mean2, scale2 = jnp.stack(mean), jnp.stack(scale)

        def act8(x):
            return x if norm is None else silu((x - mean8) * scale8 + shift)

        for p in pairs:
            here = (it > 0) if p == 0 else (it >= 0)
            for side in (0, 1):
                there = jnp.logical_and(here, (iw > 0) if side == 0 else (iw < nw - 1))
                v = act8(sl[e, p, side].astype(F32).reshape(4, 8, CH))
                v = jnp.where(there, v, 0.0).reshape(2, 16, CH)
                for t in (0, 1):
                    sf[side, 2 * p + t, pl.ds(2, 16), :] = v[t]
            v = act8(cp[e, p].astype(F32).reshape(2, 8, CH)).reshape(16, CH)
            for k in range(4):
                above, side = k >= 2, 0 if k % 2 == 1 else 1
                there = jnp.logical_and(here, (ih > 0) if above else (ih < nh - 1))
                there = jnp.logical_and(there, (iw > 0) if side == 0 else (iw < nw - 1))
                w = jnp.where(there, v[4 * k : 4 * k + 4], 0.0)
                for t in (0, 1):
                    sf[side, 2 * p + t, pl.ds(0 if above else 18, 2), :] = w[2 * t : 2 * t + 2]

        sub = lax.broadcasted_iota(jnp.int32, (2, 8, CH), 1)

        for n in range(10 * lo, 10 * hi):
            t, h = n // 10, n % 10
            there = None if t >= 2 else it > 0
            if h in (0, 9):
                row = (ih > 0) if h == 0 else (ih < nh - 1)
                there = row if there is None else jnp.logical_and(there, row)
            x = cb[e, t, h].astype(F32).reshape(2, 8, CH)
            if norm is not None:
                x = silu((x - mean2) * scale2 + shift[None])
            if there is not None:
                x = jnp.where(there, x, 0.0)
            rims = [
                jnp.stack([sf[side, t, pl.ds(2 * h + c, 1), :] for c in (0, 1)])
                for side in (0, 1)
            ]
            before = jnp.where(sub == 0, rims[0], pltpu.roll(x, 1, 1))
            after = jnp.where(sub == 7, rims[1], pltpu.roll(x, 7, 1))
            for k, v in enumerate((before, x, after)):
                ab[t, h, :, pl.ds(k * CH, CH)] = v.reshape(16, CH).astype(BF16)

    def conv(kv, t0, t1):
        total = None
        for i in range(3):
            for j in range(3):
                part = jnp.dot(
                    ab[i + t0 : i + t1, j : j + 8].reshape(128 * (t1 - t0), 3 * CH), kv[3 * i + j], preferred_element_type=F32
                )
                total = part if total is None else total + part
        return total

    def keep(e, value, t0, t1):
        cb[e, 2 + t0 : 2 + t1, 1:9] = value.reshape(t1 - t0, 8, 16, CH).astype(BF16)
        fbuf[0, 128 * t0 : 128 * t1] = value[:, :128]
        fbuf[1, 128 * t0 : 128 * t1] = value[:, 128:]

    def fold():
        def step(n, _):
            t, rows = n // 16, pl.ds(pl.multiple_of((n % 16) * 16, 16), 16)
            cols = []
            for i in range(3):
                k = [kuv[t * 3 + i, j, rows, :].astype(F32) for j in range(3)]
                cols.append((k[0], k[1] + k[2], k[0] + k[1], k[2]))
            for c in range(4):
                v = [cols[i][c] for i in range(3)]
                for r, w in enumerate((v[0], v[1] + v[2], v[0] + v[1], v[2])):
                    kuc[(r // 2) * 2 + c // 2, t, r % 2, c % 2, rows, :] = w.astype(BF16)
            return 0

        lax.fori_loop(0, 48, step, 0)

    cells = 2 * 8 * 8
    total = cells * GROUP * nt * nh * nw
    loads[0].wait()
    x = jnp.stack([xv[c].astype(F32).reshape(2, 8, 8, CH) for c in (0, 1)], axis=2)
    row = moments(x, cells * GROUP)
    keep(0, x.reshape(256, CH), 0, 2)
    pl.semaphore_wait(barrier, len(plane) + len(line))
    gather(0, 0, g1, row, plane)
    edges(0)
    arrivals = near(0)
    onward = [tile_on(0)]
    row = merge(gathered(0, 0, g1, plane), cells * GROUP)
    gather(0, 1, g2, row, line)
    onward += rims_on(0, arrivals)
    loads[2].wait()
    fold()
    row = merge(gathered(0, 1, g2, line), cells * GROUP * nh * nw)
    mean, rstd = spread_out(row, total)
    for c in onward:
        c.wait_recv()
    fill(0, (0, 4), (mean, [r * gain1[...] for r in rstd], shift1[...]))
    loads[1].wait()
    hidden = (conv(k1v, 0, 2) + bias1[...]).astype(BF16).astype(F32)

    row = moments(hidden.reshape(2, 8, 2, 8, CH), cells * GROUP)
    gather(1, 0, g3, row, pair)
    keep(1, hidden, 0, 2)
    edges(1)
    row = merge(gathered(1, 0, g3, pair), cells * GROUP)
    gather(1, 1, g4, row, chips)
    arrivals = near(1)
    onward = [tile_on(1)]
    onward += rims_on(1, arrivals)
    row = merge(gathered(1, 1, g4, chips), cells * GROUP * 2)
    mean, rstd = spread_out(row, total)
    for c in onward:
        c.wait_recv()
    fill(1, (0, 4), (mean, [r * gain2[...] for r in rstd], shift2[...]))
    loads[3].wait()
    onward = []
    for t in (0, 1):
        skip = cb[0, 2 + t, 1:9].astype(F32).reshape(128, CH)
        residual = (conv(k2v, t, t + 1) + bias2[...] + skip).astype(BF16).astype(F32)
        keep(2, residual, t, t + 1)
        onward.append(frame_on(2, t))
    edges(2)
    arrivals = near(2)
    onward += rims_on(2, arrivals)
    fill(2, (2, 4), None)
    up = bias_up[...]

    def window(t0, t1, a, b, r):
        return ab[t0:t1, a + r : a + r + 8, :, b * CH : (b + 2) * CH].reshape(128 * (t1 - t0), 2 * CH)

    def weight(a, b, i, r):
        return kuc[2 * a + b, i, r].reshape(2 * CH, CH)

    for a in (0, 1):
        for b in (0, 1):
            both = sum(jnp.dot(window(2, 4, a, b, r), weight(a, b, 2, r), preferred_element_type=F32) for r in (0, 1))
            late = sum(jnp.dot(window(2, 3, a, b, r), weight(a, b, 1, r), preferred_element_type=F32) for r in (0, 1))
            acc[2 * a + b, 0:128] = both[0:128] + up
            acc[2 * a + b, 128:256] = both[128:256] + late + up
    for c in onward:
        c.wait_recv()
    fill(2, (0, 2), None)
    for a in (0, 1):
        for b in (0, 1):
            both = sum(jnp.dot(window(0, 2, a, b, r), weight(a, b, 0, r), preferred_element_type=F32) for r in (0, 1))
            early = sum(jnp.dot(window(1, 2, a, b, r), weight(a, b, 1, r), preferred_element_type=F32) for r in (0, 1))
            done = [both[0:128] + early + acc[2 * a + b, 0:128], both[128:256] + acc[2 * a + b, 128:256]]
            for t in (0, 1):
                for half in (0, 1):
                    ob[a, half, pl.ds(256 * t + b, 128, stride=2), :] = done[t][:, half * 128 : half * 128 + 128]
        for n in range(32):
            t, h, c = n // 16, (n // 2) % 8, n % 2
            for half in (0, 1):
                out[c, t, 2 * h + a, :, pl.ds(half * 128, 128)] = ob[a, half, pl.ds(16 * n, 16), :].astype(BF16)
    for c in sends:
        c.wait_send()


def shards(sizes, latents, gain1, shift1, k1, bias1, gain2, shift2, k2, bias2, ku, bias_up):
    nt, nh, nw = sizes
    row = lambda v: v.reshape(1, CH)
    vmem = pl.BlockSpec(memory_space=pltpu.VMEM)
    hbm = pl.BlockSpec(memory_space=pl.ANY)
    s = pltpu.VMEM
    return pl.pallas_call(
        functools.partial(body, sizes),
        out_shape=pltpu.VMEM((2, 2, 16, 16, CH), BF16),
        in_specs=[hbm, vmem, vmem, hbm, vmem, vmem, vmem, hbm, vmem, hbm, vmem],
        out_specs=vmem,
        scratch_shapes=[
            s((2, 2, 64, CH), BF16),
            s((3, 4, 10, 16, CH), BF16),
            s((3, 2, 2, 32, CH), BF16),
            s((3, 16, CH), BF16),
            s((3, 4, 16, CH), BF16),
            s((3, 2, 16, CH), BF16),
            s((3, 2, 32, CH), BF16),
            s((2, 4, 20, CH), F32),
            s((4, 10, 16, 3 * CH), BF16),
            s((9, 3 * CH, CH), BF16),
            s((9, 3 * CH, CH), BF16),
            s((9, 3, CH, CH), BF16),
            s((4, 3, 2, 2, CH, CH), BF16),
            s((2, 256, 128), F32),
            s((4, 256, CH), F32),
            s((2, 2, 512, 128), F32),
            s((nh * nw, 1, 128), F32),
            s((nt, 1, 128), F32),
            s((2, 1, 128), F32),
            s((nt * nh * nw // 2, 1, 128), F32),
            pltpu.SemaphoreType.DMA((4,)),
            pltpu.SemaphoreType.DMA((3, 14)),
            pltpu.SemaphoreType.DMA((3, 14)),
            pltpu.SemaphoreType.DMA((2, 2)),
            pltpu.SemaphoreType.DMA((2, 2)),
        ],
        compiler_params=pltpu.CompilerParams(
            collective_id=0, has_side_effects=True, vmem_limit_bytes=62 * 2**20
        ),
        name="upblock",
    )(
        latents.reshape(2, 2, 64, CH), row(gain1), row(shift1), k1.reshape(9, 3 * CH, CH), row(bias1),
        row(gain2), row(shift2), k2.reshape(9, 3 * CH, CH), row(bias2), ku.reshape(9, 3, CH, CH), row(bias_up),
    )


def solution(mesh):
    sizes = tuple(mesh.shape[a] for a in AXES)
    in_specs = (P(None, "tm", "ha", "wa", None),) + (P(),) * 10
    return jax.shard_map(
        functools.partial(shards, sizes),
        mesh=mesh,
        in_specs=in_specs,
        out_specs=P(None, "tm", "ha", "wa", None),
        check_vma=False,
    )
```

profile of v0, /device:TPU:1, one launch (start us, length us, event | category | flops | bytes accessed | tf_op | source)
XLA Modules:
  0.0 45.7 jit_solution(13407493855929752284)
XLA Ops:
  0.0 44.9 %upblock.1 = bf16[2,2,16,16,256]{4,3,2,1,0:T(8,128)(2,1)S(1)} custom-call(bf16[2,2,64,256]{3,2,1,0:T(8,128)(2,1)} %bitcast.14, f32[1,256]{1,0:T(1,128)} %bitcast.15, f32[1,256]{1,0:T(1,128)} %bitcast.16, bf16[9,768,256]{2,1,0:T(8,128)(2,1)} %bitcast.11, f32[1,256]{1,0:T(1,128)} %bitcast.17, f32[1,256]{1,0:T(1,128)} %bitcast.18, f32[1,256]{1,0:T(1,128)} %bitcast.19, ...), custom_call_target="tpu_custom_call" | custom-call | tf_op jit(solution)/shard_map/upblock/pallas_call | solution.py:352
  44.9 0.8 %copy.13 = bf16[2,2,16,16,256]{4,3,2,1,0:T(8,128)(2,1)} copy(bf16[2,2,16,16,256]{4,3,2,1,0:T(8,128)(2,1)S(1)} %upblock.1) | data formatting | bytes 1048576
where the time goes:
time: 45.8 us; the launch traced here: 45.7 us
  Pallas kernels  44.9 us (98%)
  local copies, waits for them, and re-layouts  0.8 us (2%)
    pallas_call x1, Pallas kernels, shards(): pl.pallas_call(functools.partial(body, sizes), out_shape=pltpu.VMEM((2, 2...  44.9 us

commit v1 on v0

--- a/solution.py
+++ b/solution.py
@@ -67,15 +67,17 @@
 
 
 def body(sizes, lat, gain1, shift1, k1, bias1, gain2, shift2, k2, bias2, ku, bias_up, out,
-         xv, cb, sl, sx, xr, cp, ss, sf, ab, k1v, k2v, kuv, kuc, fbuf, acc, ob, g1, g2, g3, g4,
+         xv, cb, sl, sx, xr, cp, ss, sf, ab, k1v, k2v, kuv, kuc, fbuf, acc, ob, g1, g2, g3, g4, g5, g6,
          lsem, ssem, rsem, gsend, grecv):
     nt, nh, nw = sizes
     it, ih, iw = (lax.axis_index(a) for a in AXES)
+    core = lax.rem(ih, 2)
 
     def at(dt, dh, dw):
         if dh is None:
             return (it, ih + 1 - 2 * lax.rem(ih, 2), iw)
-        return (lax.rem(it + dt % nt, nt), lax.rem(ih + dh % nh, nh), lax.rem(iw + dw % nw, nw))
+        dt = dt % nt if isinstance(dt, int) else dt
+        return (lax.rem(it + dt, nt), lax.rem(ih + dh % nh, nh), lax.rem(iw + dw % nw, nw))
 
     def ring(d, n):
         return min(d, n - d)
@@ -88,8 +90,8 @@
 
     pair = [(0, None, 0)]
     chips = sorted(
-        [(a, 2 * b, c) for a in range(nt) for b in range(nh // 2) for c in range(nw) if a or b or c],
-        key=lambda o: -(ring(o[0], nt) + ring(o[1], nh) // 2 + ring(o[2], nw)),
+        [(a, 2 * b, c) for a in range(nt // 2) for b in range(nh // 2) for c in range(nw) if a or b or c],
+        key=lambda o: -(max(ring(o[0], nt), nt // 2 - o[0]) + ring(o[1], nh) // 2 + ring(o[2], nw)),
     )
 
     loads = [
@@ -113,40 +115,61 @@
         sends.append(c)
         return c
 
-    def edges(e):
+    def columns(e, t0, t1):
         for half in (0, 1):
-            cols = pl.ds(half * 128, 128)
-            left = fbuf[half, pl.ds(0, 32, stride=8), :]
-            right = fbuf[half, pl.ds(7, 32, stride=8), :]
-            ss[e, 0, :, cols] = left.astype(BF16)
-            ss[e, 1, :, cols] = right.astype(BF16)
+            for side in (0, 1):
+                column = fbuf[half, pl.ds(128 * t0 + 7 * side, 16 * (t1 - t0), stride=8), :]
+                ss[e, side, pl.ds(16 * t0, 16 * (t1 - t0)), pl.ds(half * 128, 128)] = column.astype(BF16)
+
+    def corners(e):
+        for half in (0, 1):
+            sides = [fbuf[half, pl.ds(7 * side, 32, stride=8), :] for side in (0, 1)]
             parts = []
             for h in (0, 14):
-                for side in (left, right):
+                for side in sides:
                     parts += [side[h : h + 2], side[16 + h : 18 + h]]
-            sx[e, :, cols] = jnp.concatenate(parts, axis=0).astype(BF16)
-
-    def near(e):
-        own = pl.ds(2, 2)
+            sx[e, :, pl.ds(half * 128, 128)] = jnp.concatenate(parts, axis=0).astype(BF16)
+
+    def rows_out(e, t0, t1, slot):
+        own = pl.ds(2 + t0, t1 - t0)
         return [
-            send(e, 0, cb.at[e, own, 1], cb.at[e, own, 9], (0, -1, 0)),
-            send(e, 1, cb.at[e, own, 8], cb.at[e, own, 0], (0, 1, 0)),
-            send(e, 2, ss.at[e, 0], sl.at[e, 1, 1], (0, 0, -1)),
-            send(e, 3, ss.at[e, 1], sl.at[e, 1, 0], (0, 0, 1)),
-            send(e, 4, sx.at[e], xr.at[e, 0], (0, -1, -1)),
-            send(e, 5, sx.at[e], xr.at[e, 1], (0, -1, 1)),
-            send(e, 6, sx.at[e], xr.at[e, 2], (0, 1, -1)),
-            send(e, 7, sx.at[e], xr.at[e, 3], (0, 1, 1)),
+            send(e, slot, cb.at[e, own, 1], cb.at[e, own, 9], (0, -1, 0)),
+            send(e, slot + 1, cb.at[e, own, 8], cb.at[e, own, 0], (0, 1, 0)),
         ]
 
-    def tile_on(e):
-        return send(e, 8, cb.at[e, pl.ds(2, 2), pl.ds(1, 8)], cb.at[e, pl.ds(0, 2), pl.ds(1, 8)], (1, 0, 0))
-
-    def frame_on(e, t):
+    def columns_out(e, t0, t1, slot):
+        part = pl.ds(16 * t0, 16 * (t1 - t0))
+        return [
+            send(e, slot, ss.at[e, 0, part], sl.at[e, 1, 1, part], (0, 0, -1)),
+            send(e, slot + 1, ss.at[e, 1, part], sl.at[e, 1, 0, part], (0, 0, 1)),
+        ]
+
+    def corners_out(e):
+        return [
+            send(e, 4 + 2 * a + b, sx.at[e], xr.at[e, 2 * a + b], (0, 2 * a - 1, 2 * b - 1))
+            for a in (0, 1)
+            for b in (0, 1)
+        ]
+
+    def frames_on(e, t0, t1, slot):
         rows = pl.ds(1, 8)
-        return send(e, 8 if t == 0 else 13, cb.at[e, 2 + t, rows], cb.at[e, t, rows], (1, 0, 0))
-
-    def rims_on(e, arrivals):
+        return [send(e, slot, cb.at[e, pl.ds(2 + t0, t1 - t0), rows], cb.at[e, pl.ds(t0, t1 - t0), rows], (1, 0, 0))]
+
+    def rows_on(e, t0, t1, slot, arrivals):
+        for c in arrivals:
+            c.wait_recv()
+        return [
+            send(e, slot + k, cb.at[e, pl.ds(2 + t0, t1 - t0), h], cb.at[e, pl.ds(t0, t1 - t0), h], (1, 0, 0))
+            for k, h in enumerate((0, 9))
+        ]
+
+    def columns_on(e, t0, t1, slot, arrivals):
+        for c in arrivals:
+            c.wait_recv()
+        part = pl.ds(16 * t0, 16 * (t1 - t0))
+        return [send(e, slot + k, sl.at[e, 1, k, part], sl.at[e, 0, k, part], (1, 0, 0)) for k in (0, 1)]
+
+    def corners_on(e, arrivals):
         for c in arrivals:
             c.wait_recv()
         block = lax.broadcasted_iota(jnp.int32, (16, CH), 0) // 4
@@ -155,13 +178,18 @@
             block == 0, tiles[0], jnp.where(block == 1, tiles[1], jnp.where(block == 2, tiles[2], tiles[3]))
         )
         cp[e, 1] = picked.astype(BF16)
-        prev, own = pl.ds(0, 2), pl.ds(2, 2)
-        return [
-            send(e, 9, cb.at[e, own, 0], cb.at[e, prev, 0], (1, 0, 0)),
-            send(e, 10, cb.at[e, own, 9], cb.at[e, prev, 9], (1, 0, 0)),
-            send(e, 11, sl.at[e, 1], sl.at[e, 0], (1, 0, 0)),
-            send(e, 12, cp.at[e, 1], cp.at[e, 0], (1, 0, 0)),
-        ]
+        return [send(e, 12, cp.at[e, 1], cp.at[e, 0], (1, 0, 0))]
+
+    def rims_out(e):
+        rows = rows_out(e, 0, 2, 0)
+        tile = frames_on(e, 0, 2, 8)
+        columns(e, 0, 2)
+        cols = columns_out(e, 0, 2, 2)
+        corners(e)
+        return tile, (rows, cols, corners_out(e))
+
+    def rims_on(e, near):
+        return rows_on(e, 0, 2, 9, near[0]) + columns_on(e, 0, 2, 13, near[1]) + corners_on(e, near[2])
 
     def gather(e, phase, buf, row, offsets):
         buf[0] = row
@@ -269,12 +297,10 @@
     keep(0, x.reshape(256, CH), 0, 2)
     pl.semaphore_wait(barrier, len(plane) + len(line))
     gather(0, 0, g1, row, plane)
-    edges(0)
-    arrivals = near(0)
-    onward = [tile_on(0)]
+    onward, near = rims_out(0)
     row = merge(gathered(0, 0, g1, plane), cells * GROUP)
     gather(0, 1, g2, row, line)
-    onward += rims_on(0, arrivals)
+    onward += rims_on(0, near)
     loads[2].wait()
     fold()
     row = merge(gathered(0, 1, g2, line), cells * GROUP * nh * nw)
@@ -288,27 +314,54 @@
     row = moments(hidden.reshape(2, 8, 2, 8, CH), cells * GROUP)
     gather(1, 0, g3, row, pair)
     keep(1, hidden, 0, 2)
-    edges(1)
+    onward, near = rims_out(1)
     row = merge(gathered(1, 0, g3, pair), cells * GROUP)
-    gather(1, 1, g4, row, chips)
-    arrivals = near(1)
-    onward = [tile_on(1)]
-    onward += rims_on(1, arrivals)
+    g5[0] = row
+    far = pltpu.make_async_remote_copy(
+        src_ref=g5.at[0], dst_ref=g4.at[0], send_sem=gsend.at[1, 2], recv_sem=grecv.at[1, 2],
+        device_id=at(nt // 2, 0, 0), device_id_type=MESH)
+
+    @pl.when(core == 0)
+    def _():
+        g4[0] = row
+
+    @pl.when(core == 1)
+    def _():
+        far.start()
+
+    for slot, o in enumerate(chips):
+        pltpu.make_async_remote_copy(
+            src_ref=g5.at[0], dst_ref=g4.at[1 + slot], send_sem=gsend.at[1, 1], recv_sem=grecv.at[1, 1],
+            device_id=at(o[0] + nt // 2 * core, o[1], o[2]), device_id_type=MESH).start()
+    onward += rims_on(1, near)
+
+    @pl.when(core == 1)
+    def _():
+        far.wait_recv()
+        far.wait_send()
+
     row = merge(gathered(1, 1, g4, chips), cells * GROUP * 2)
+    gather(1, 3, g6, row, pair)
+    row = merge(gathered(1, 3, g6, pair), cells * GROUP * nt * nh * nw // 2)
     mean, rstd = spread_out(row, total)
     for c in onward:
         c.wait_recv()
     fill(1, (0, 4), (mean, [r * gain2[...] for r in rstd], shift2[...]))
     loads[3].wait()
-    onward = []
+    onward, near = [], []
     for t in (0, 1):
         skip = cb[0, 2 + t, 1:9].astype(F32).reshape(128, CH)
         residual = (conv(k2v, t, t + 1) + bias2[...] + skip).astype(BF16).astype(F32)
         keep(2, residual, t, t + 1)
-        onward.append(frame_on(2, t))
-    edges(2)
-    arrivals = near(2)
-    onward += rims_on(2, arrivals)
+        onward += frames_on(2, t, t + 1, 8 + 13 * t)
+        near.append(rows_out(2, t, t + 1, 16 * t))
+        columns(2, t, t + 1)
+        near.append(columns_out(2, t, t + 1, 2 + 16 * t))
+    corners(2)
+    near.append(corners_out(2))
+    onward += rows_on(2, 0, 1, 9, near[0]) + columns_on(2, 0, 1, 13, near[1])
+    onward += rows_on(2, 1, 2, 22, near[2]) + columns_on(2, 1, 2, 24, near[3])
+    onward += corners_on(2, near[4])
     fill(2, (2, 4), None)
     up = bias_up[...]
 
@@ -374,12 +427,14 @@
             s((nh * nw, 1, 128), F32),
             s((nt, 1, 128), F32),
             s((2, 1, 128), F32),
-            s((nt * nh * nw // 2, 1, 128), F32),
+            s((nt * nh * nw // 4, 1, 128), F32),
+            s((1, 1, 128), F32),
+            s((2, 1, 128), F32),
             pltpu.SemaphoreType.DMA((4,)),
-            pltpu.SemaphoreType.DMA((3, 14)),
-            pltpu.SemaphoreType.DMA((3, 14)),
-            pltpu.SemaphoreType.DMA((2, 2)),
-            pltpu.SemaphoreType.DMA((2, 2)),
+            pltpu.SemaphoreType.DMA((3, 26)),
+            pltpu.SemaphoreType.DMA((3, 26)),
+            pltpu.SemaphoreType.DMA((2, 4)),
+            pltpu.SemaphoreType.DMA((2, 4)),
         ],
         compiler_params=pltpu.CompilerParams(
             collective_id=0, has_side_effects=True, vmem_limit_bytes=62 * 2**20

time: 45.8 us -> 44.5 us (0.972)
  Pallas kernels: 44.9 us -> 43.2 us
    pallas_call x1, Pallas kernels: 44.9 us -> 43.2 us  [shards(): pl.pallas_call(functools.partial(body, sizes), out_shape=pltpu.VMEM((2, 2...]
where the time goes in v1:
time: 44.5 us; the launch traced here: 44 us
  Pallas kernels  43.2 us (97%)
  local copies, waits for them, and re-layouts  0.8 us (2%)
    pallas_call x1, Pallas kernels, shards(): pl.pallas_call(functools.partial(body, sizes), out_shape=pltpu.VMEM((2, 2...  43.2 us

profile of v1, /device:TPU:1, one launch (start us, length us, event | category | flops | bytes accessed | tf_op | source)
XLA Modules:
  0.0 44.0 jit_solution(1356484997041714135)
XLA Ops:
  0.0 43.2 %upblock.1 = bf16[2,2,16,16,256]{4,3,2,1,0:T(8,128)(2,1)S(1)} custom-call(bf16[2,2,64,256]{3,2,1,0:T(8,128)(2,1)} %bitcast.14, f32[1,256]{1,0:T(1,128)} %bitcast.15, f32[1,256]{1,0:T(1,128)} %bitcast.16, bf16[9,768,256]{2,1,0:T(8,128)(2,1)} %bitcast.11, f32[1,256]{1,0:T(1,128)} %bitcast.17, f32[1,256]{1,0:T(1,128)} %bitcast.18, f32[1,256]{1,0:T(1,128)} %bitcast.19, ...), custom_call_target="tpu_custom_call" | custom-call | tf_op jit(solution)/shard_map/upblock/pallas_call | solution.py:405
  43.2 0.8 %copy.13 = bf16[2,2,16,16,256]{4,3,2,1,0:T(8,128)(2,1)} copy(bf16[2,2,16,16,256]{4,3,2,1,0:T(8,128)(2,1)S(1)} %upblock.1) | data formatting | bytes 1048576

commit v2 on v1

--- a/solution.py
+++ b/solution.py
@@ -71,13 +71,18 @@
          lsem, ssem, rsem, gsend, grecv):
     nt, nh, nw = sizes
     it, ih, iw = (lax.axis_index(a) for a in AXES)
-    core = lax.rem(ih, 2)
+    core = lax.bitwise_and(ih, 1)
+
+    def turn(index, n):
+        return lax.bitwise_and(index, n - 1) if n & (n - 1) == 0 else lax.rem(index, n)
+
+    places = [[turn(i + d, n) if d else i for d in range(n)] for i, n in ((it, nt), (ih, nh), (iw, nw))]
+    halfway = [turn(i + nt // 2 * core, nt) for i in places[0]]
 
     def at(dt, dh, dw):
         if dh is None:
-            return (it, ih + 1 - 2 * lax.rem(ih, 2), iw)
-        dt = dt % nt if isinstance(dt, int) else dt
-        return (lax.rem(it + dt, nt), lax.rem(ih + dh % nh, nh), lax.rem(iw + dw % nw, nw))
+            return (it, ih + 1 - 2 * core, iw)
+        return (places[0][dt % nt], places[1][dh % nh], places[2][dw % nw])
 
     def ring(d, n):
         return min(d, n - d)
@@ -180,9 +185,9 @@
         cp[e, 1] = picked.astype(BF16)
         return [send(e, 12, cp.at[e, 1], cp.at[e, 0], (1, 0, 0))]
 
-    def rims_out(e):
+    def rims_out(e, tile_now=True):
         rows = rows_out(e, 0, 2, 0)
-        tile = frames_on(e, 0, 2, 8)
+        tile = frames_on(e, 0, 2, 8) if tile_now else []
         columns(e, 0, 2)
         cols = columns_out(e, 0, 2, 2)
         corners(e)
@@ -209,7 +214,6 @@
 
     def fill(e, frames, norm):
         lo, hi = frames
-        pairs = [p for p in (0, 1) if lo <= 2 * p < hi]
         if norm is not None:
             mean, scale, shift = norm
             parity = lax.broadcasted_iota(jnp.int32, (8, CH), 0) % 2 == 0
@@ -220,22 +224,20 @@
         def act8(x):
             return x if norm is None else silu((x - mean8) * scale8 + shift)
 
-        for p in pairs:
+        for t in range(lo, hi):
+            p, tt = t // 2, t % 2
             here = (it > 0) if p == 0 else (it >= 0)
             for side in (0, 1):
                 there = jnp.logical_and(here, (iw > 0) if side == 0 else (iw < nw - 1))
-                v = act8(sl[e, p, side].astype(F32).reshape(4, 8, CH))
-                v = jnp.where(there, v, 0.0).reshape(2, 16, CH)
-                for t in (0, 1):
-                    sf[side, 2 * p + t, pl.ds(2, 16), :] = v[t]
+                v = act8(sl[e, p, side, pl.ds(16 * tt, 16)].astype(F32).reshape(2, 8, CH))
+                sf[side, t, pl.ds(2, 16), :] = jnp.where(there, v, 0.0).reshape(16, CH)
             v = act8(cp[e, p].astype(F32).reshape(2, 8, CH)).reshape(16, CH)
             for k in range(4):
                 above, side = k >= 2, 0 if k % 2 == 1 else 1
                 there = jnp.logical_and(here, (ih > 0) if above else (ih < nh - 1))
                 there = jnp.logical_and(there, (iw > 0) if side == 0 else (iw < nw - 1))
-                w = jnp.where(there, v[4 * k : 4 * k + 4], 0.0)
-                for t in (0, 1):
-                    sf[side, 2 * p + t, pl.ds(0 if above else 18, 2), :] = w[2 * t : 2 * t + 2]
+                at_k = 4 * k + 2 * tt
+                sf[side, t, pl.ds(0 if above else 18, 2), :] = jnp.where(there, v[at_k : at_k + 2], 0.0)
 
         sub = lax.broadcasted_iota(jnp.int32, (2, 8, CH), 1)
 
@@ -314,7 +316,7 @@
     row = moments(hidden.reshape(2, 8, 2, 8, CH), cells * GROUP)
     gather(1, 0, g3, row, pair)
     keep(1, hidden, 0, 2)
-    onward, near = rims_out(1)
+    onward, near = rims_out(1, False)
     row = merge(gathered(1, 0, g3, pair), cells * GROUP)
     g5[0] = row
     far = pltpu.make_async_remote_copy(
@@ -332,8 +334,8 @@
     for slot, o in enumerate(chips):
         pltpu.make_async_remote_copy(
             src_ref=g5.at[0], dst_ref=g4.at[1 + slot], send_sem=gsend.at[1, 1], recv_sem=grecv.at[1, 1],
-            device_id=at(o[0] + nt // 2 * core, o[1], o[2]), device_id_type=MESH).start()
-    onward += rims_on(1, near)
+            device_id=(halfway[o[0]],) + at(*o)[1:], device_id_type=MESH).start()
+    onward += frames_on(1, 0, 2, 8) + rims_on(1, near)
 
     @pl.when(core == 1)
     def _():
@@ -348,6 +350,8 @@
         c.wait_recv()
     fill(1, (0, 4), (mean, [r * gain2[...] for r in rstd], shift2[...]))
     loads[3].wait()
+    earlier = list(sends)
+    sends.clear()
     onward, near = [], []
     for t in (0, 1):
         skip = cb[0, 2 + t, 1:9].astype(F32).reshape(128, CH)
@@ -359,9 +363,9 @@
         near.append(columns_out(2, t, t + 1, 2 + 16 * t))
     corners(2)
     near.append(corners_out(2))
-    onward += rows_on(2, 0, 1, 9, near[0]) + columns_on(2, 0, 1, 13, near[1])
-    onward += rows_on(2, 1, 2, 22, near[2]) + columns_on(2, 1, 2, 24, near[3])
-    onward += corners_on(2, near[4])
+    first = onward[:1] + rows_on(2, 0, 1, 9, near[0]) + columns_on(2, 0, 1, 13, near[1])
+    first += corners_on(2, near[4])
+    second = onward[1:] + rows_on(2, 1, 2, 22, near[2]) + columns_on(2, 1, 2, 24, near[3])
     fill(2, (2, 4), None)
     up = bias_up[...]
 
@@ -377,14 +381,26 @@
             late = sum(jnp.dot(window(2, 3, a, b, r), weight(a, b, 1, r), preferred_element_type=F32) for r in (0, 1))
             acc[2 * a + b, 0:128] = both[0:128] + up
             acc[2 * a + b, 128:256] = both[128:256] + late + up
-    for c in onward:
+    for c in earlier:
+        c.wait_send()
+    for c in first:
         c.wait_recv()
-    fill(2, (0, 2), None)
+    fill(2, (0, 1), None)
     for a in (0, 1):
         for b in (0, 1):
-            both = sum(jnp.dot(window(0, 2, a, b, r), weight(a, b, 0, r), preferred_element_type=F32) for r in (0, 1))
-            early = sum(jnp.dot(window(1, 2, a, b, r), weight(a, b, 1, r), preferred_element_type=F32) for r in (0, 1))
-            done = [both[0:128] + early + acc[2 * a + b, 0:128], both[128:256] + acc[2 * a + b, 128:256]]
+            acc[2 * a + b, 0:128] += sum(
+                jnp.dot(window(0, 1, a, b, r), weight(a, b, 0, r), preferred_element_type=F32) for r in (0, 1)
+            )
+    for c in second:
+        c.wait_recv()
+    fill(2, (1, 2), None)
+    for a in (0, 1):
+        for b in (0, 1):
+            late, early = (
+                sum(jnp.dot(window(1, 2, a, b, r), weight(a, b, i, r), preferred_element_type=F32) for r in (0, 1))
+                for i in (0, 1)
+            )
+            done = [early + acc[2 * a + b, 0:128], late + acc[2 * a + b, 128:256]]
             for t in (0, 1):
                 for half in (0, 1):
                     ob[a, half, pl.ds(256 * t + b, 128, stride=2), :] = done[t][:, half * 128 : half * 128 + 128]
@@ -421,9 +437,9 @@
             s((9, 3 * CH, CH), BF16),
             s((9, 3, CH, CH), BF16),
             s((4, 3, 2, 2, CH, CH), BF16),
-            s((2, 256, 128), F32),
+            s((2, 264, 128), F32),
             s((4, 256, CH), F32),
-            s((2, 2, 512, 128), F32),
+            s((2, 2, 520, 128), F32),
             s((nh * nw, 1, 128), F32),
             s((nt, 1, 128), F32),
             s((2, 1, 128), F32),

time: 44.5 us -> 44 us (0.989)
  no operation moved by 1% of the time
where the time goes in v2:
time: 44 us; the launch traced here: 43.9 us
  Pallas kernels  43.1 us (98%)
  local copies, waits for them, and re-layouts  0.8 us (2%)
    pallas_call x1, Pallas kernels, shards(): pl.pallas_call(functools.partial(body, sizes), out_shape=pltpu.VMEM((2, 2...  43.1 us

profile of v2, /device:TPU:1, one launch (start us, length us, event | category | flops | bytes accessed | tf_op | source)
XLA Modules:
  0.0 43.9 jit_solution(7243990816790322286)
XLA Ops:
  0.0 43.1 %upblock.1 = bf16[2,2,16,16,256]{4,3,2,1,0:T(8,128)(2,1)S(1)} custom-call(bf16[2,2,64,256]{3,2,1,0:T(8,128)(2,1)} %bitcast.14, f32[1,256]{1,0:T(1,128)} %bitcast.15, f32[1,256]{1,0:T(1,128)} %bitcast.16, bf16[9,768,256]{2,1,0:T(8,128)(2,1)} %bitcast.11, f32[1,256]{1,0:T(1,128)} %bitcast.17, f32[1,256]{1,0:T(1,128)} %bitcast.18, f32[1,256]{1,0:T(1,128)} %bitcast.19, ...), custom_call_target="tpu_custom_call" | custom-call | tf_op jit(solution)/shard_map/upblock/pallas_call | solution.py:421
  43.1 0.8 %copy.13 = bf16[2,2,16,16,256]{4,3,2,1,0:T(8,128)(2,1)} copy(bf16[2,2,16,16,256]{4,3,2,1,0:T(8,128)(2,1)S(1)} %upblock.1) | data formatting | bytes 1048576

commit v3 on v2

--- a/solution.py
+++ b/solution.py
@@ -105,7 +105,7 @@
     ]
     loads[0].start()
     barrier = pltpu.get_barrier_semaphore()
-    for o in plane + line:
+    for o in sorted(plane + line, key=lambda o: -(2 * ring(o[0], nt) + ring(o[1], nh) + 2 * ring(o[2], nw))):
         pl.semaphore_signal(barrier, inc=1, device_id=at(*o), device_id_type=MESH)
     for c in loads[1:]:
         c.start()
@@ -190,8 +190,7 @@
         tile = frames_on(e, 0, 2, 8) if tile_now else []
         columns(e, 0, 2)
         cols = columns_out(e, 0, 2, 2)
-        corners(e)
-        return tile, (rows, cols, corners_out(e))
+        return tile, rows, cols
 
     def rims_on(e, near):
         return rows_on(e, 0, 2, 9, near[0]) + columns_on(e, 0, 2, 13, near[1]) + corners_on(e, near[2])
@@ -296,10 +295,12 @@
     loads[0].wait()
     x = jnp.stack([xv[c].astype(F32).reshape(2, 8, 8, CH) for c in (0, 1)], axis=2)
     row = moments(x, cells * GROUP)
-    keep(0, x.reshape(256, CH), 0, 2)
     pl.semaphore_wait(barrier, len(plane) + len(line))
     gather(0, 0, g1, row, plane)
-    onward, near = rims_out(0)
+    keep(0, x.reshape(256, CH), 0, 2)
+    onward, rows, cols = rims_out(0)
+    corners(0)
+    near = rows, cols, corners_out(0)
     row = merge(gathered(0, 0, g1, plane), cells * GROUP)
     gather(0, 1, g2, row, line)
     onward += rims_on(0, near)
@@ -316,7 +317,7 @@
     row = moments(hidden.reshape(2, 8, 2, 8, CH), cells * GROUP)
     gather(1, 0, g3, row, pair)
     keep(1, hidden, 0, 2)
-    onward, near = rims_out(1, False)
+    onward, rows, cols = rims_out(1, False)
     row = merge(gathered(1, 0, g3, pair), cells * GROUP)
     g5[0] = row
     far = pltpu.make_async_remote_copy(
@@ -335,7 +336,9 @@
         pltpu.make_async_remote_copy(
             src_ref=g5.at[0], dst_ref=g4.at[1 + slot], send_sem=gsend.at[1, 1], recv_sem=grecv.at[1, 1],
             device_id=(halfway[o[0]],) + at(*o)[1:], device_id_type=MESH).start()
-    onward += frames_on(1, 0, 2, 8) + rims_on(1, near)
+    onward += frames_on(1, 0, 2, 8)
+    corners(1)
+    onward += rims_on(1, (rows, cols, corners_out(1)))
 
     @pl.when(core == 1)
     def _():

time: 44 us -> 44 us (level)
  no operation moved by 1% of the time
where the time goes in v3:
time: 44 us; the launch traced here: 43.9 us
  Pallas kernels  43.1 us (98%)
  local copies, waits for them, and re-layouts  0.8 us (2%)
    pallas_call x1, Pallas kernels, shards(): pl.pallas_call(functools.partial(body, sizes), out_shape=pltpu.VMEM((2, 2...  43.1 us

profile of v3, /device:TPU:1, one launch (start us, length us, event | category | flops | bytes accessed | tf_op | source)
XLA Modules:
  0.0 43.9 jit_solution(3089472583481358386)
XLA Ops:
  0.0 43.1 %upblock.1 = bf16[2,2,16,16,256]{4,3,2,1,0:T(8,128)(2,1)S(1)} custom-call(bf16[2,2,64,256]{3,2,1,0:T(8,128)(2,1)} %bitcast.14, f32[1,256]{1,0:T(1,128)} %bitcast.15, f32[1,256]{1,0:T(1,128)} %bitcast.16, bf16[9,768,256]{2,1,0:T(8,128)(2,1)} %bitcast.11, f32[1,256]{1,0:T(1,128)} %bitcast.17, f32[1,256]{1,0:T(1,128)} %bitcast.18, f32[1,256]{1,0:T(1,128)} %bitcast.19, ...), custom_call_target="tpu_custom_call" | custom-call | tf_op jit(solution)/shard_map/upblock/pallas_call | solution.py:424
  43.1 0.8 %copy.13 = bf16[2,2,16,16,256]{4,3,2,1,0:T(8,128)(2,1)} copy(bf16[2,2,16,16,256]{4,3,2,1,0:T(8,128)(2,1)S(1)} %upblock.1) | data formatting | bytes 1048576
